TPU v7x, 32 devices: a whole 2x2x4 slice. The times are simulated.
32 devices in a mesh: bx: 8 (over y, x, core), by: 4 (over z).
Axes of the slice: x: 2, y: 2, z: 4, core: 2. Of those that a mesh axis runs over, the one named last changes fastest.
Arguments:
- adjoint_start: float32 [6, 128, 64, 128], P(None, 'bx', 'by'), may hold values from -6 to 6
- objective_grad: float32 [6, 128, 64, 128], P(None, 'bx', 'by'), may hold values from -4 to 4
- spectral_radius: float32 [3, 128, 64, 128], P(None, 'bx', 'by'), may hold values from 0.5 to 4
- local_step: float32 [128, 64, 128], P('bx', 'by'), may hold values from 0.02 to 0.12
- flux_jacobian: float32 [3, 6, 6], replicated, may hold values from -2.5 to 2.5
- face_orient: int32 [8, 2], P('bx'), may hold values from 0 to 1, as said below
- wall_count: int32 [8, 4], P('bx', 'by'), may hold values from 0 to 256
- face_patch: int32 [128, 64], P('bx', 'by'), may hold values from 0 to 127
- face_area: float32 [128, 64], P('bx', 'by'), may hold values from 1 to 10
- force_weight: float32 [6], replicated, may hold values from -3 to 3
Outputs:
- adjoint_next: float32 [6, 128, 64, 128], P(None, 'bx', 'by')
- patch_force: float32 [128], P(('bx', 'by'))
Inputs may be any that keep to these rules, and one draw needn't show every extreme that they name: face_orient[a, 1] equals face_orient[a + 1, 0]; a 1 marks a face between block rows whose matched cells run in reverse order along the third direction.
All inputs are finite; a program needn't handle non-finite values.
Results may differ from a plain program's by a relative error of at most 0.00012.
Values sent between devices are 32-bit elements; how exact they have to be, the bound alone decides.
A program may use at most 64 MiB of HBM per device.

v0:
```python
import jax
import jax.numpy as jnp
from jax import lax
from jax.sharding import PartitionSpec as P

P_DEV = 4


EPS = 0.1


def with_halo(shard, sides, width):
    for axis, dim in sides:
        devices, length = (lax.axis_size(axis), shard.shape[dim])
        up = [(i, (i + 1) % devices) for i in range(devices - 1)]
        down = [(j, i) for i, j in up]
        last = lax.slice_in_dim(shard, length - width, length, axis=dim)
        first = lax.slice_in_dim(shard, 0, width, axis=dim)
        before = lax.ppermute(last, axis, up)
        after = lax.ppermute(first, axis, down)
        shard = jnp.concatenate([before, shard, after], axis=dim)
    return shard


def flip_rims(padded, width, low_flag, high_flag):
    lower = padded[:, :width]
    upper = padded[:, padded.shape[1] - width :]
    middle = padded[:, width : padded.shape[1] - width]
    lower = jnp.where(low_flag == 1, jnp.flip(lower, 3), lower)
    upper = jnp.where(high_flag == 1, jnp.flip(upper, 3), upper)
    return jnp.concatenate([lower, middle, upper], axis=1)


def transpose_apply(matrix, field):
    return jnp.einsum("fg,fxyz->gxyz", matrix, field, precision=lax.Precision.HIGHEST)


def operate(extended, radius, flux_jacobian):
    rows_i = extended.shape[1] - 4
    rows_j = extended.shape[2] - 4
    center = extended[:, 2 : 2 + rows_i, 2 : 2 + rows_j]
    depth = center.shape[3]
    padded_k = jnp.pad(center, ((0, 0), (0, 0), (0, 0), (2, 2)))

    def along_first(offset):
        return extended[:, 2 + offset : 2 + offset + rows_i, 2 : 2 + rows_j]

    def along_second(offset):
        return extended[:, 2 : 2 + rows_i, 2 + offset : 2 + offset + rows_j]

    def along_third(offset):
        return padded_k[:, :, :, 2 + offset : 2 + offset + depth]

    summed = jnp.zeros_like(center)
    for direction, slicer in ((0, along_first), (1, along_second), (2, along_third)):
        front_one = slicer(1)
        back_one = slicer(-1)
        fourth = slicer(2) - 4.0 * front_one + 6.0 * center - 4.0 * back_one + slicer(-2)
        if direction == 2:
            coupled = transpose_apply(flux_jacobian[direction], front_one + back_one)
        else:
            coupled = transpose_apply(flux_jacobian[direction], front_one - back_one)
        summed = summed + radius[direction] * (0.5 * coupled + EPS * fourth)
    return summed


def local(
    adjoint_start,
    objective_grad,
    spectral_radius,
    local_step,
    flux_jacobian,
    face_orient,
    wall_count,
    face_patch,
    face_area,
    force_weight,
):
    rows_i = adjoint_start.shape[1]
    rows_j = adjoint_start.shape[2]
    patch_total = P_DEV * lax.axis_size("bx") * lax.axis_size("by")
    low_flag = face_orient[0, 0]
    high_flag = face_orient[0, 1]
    position = jnp.arange(rows_i)[:, None] * rows_j + jnp.arange(rows_j)[None, :]
    live = (position < wall_count[0, 0]).astype(jnp.float32)
    wall_adjoint = jnp.einsum(
        "f,fxy->xy", force_weight, adjoint_start[:, :, :, 0], precision=lax.Precision.HIGHEST
    )
    weighted_area = (live * face_area).reshape(-1)
    wall_value = weighted_area * wall_adjoint.reshape(-1)
    patch_ids = face_patch.reshape(-1)
    table = (patch_ids[:, None] == jnp.arange(patch_total)[None, :]).astype(jnp.float32)
    local_sum = jnp.dot(wall_value, table, precision=lax.Precision.HIGHEST)
    local_area = jnp.dot(weighted_area, table, precision=lax.Precision.HIGHEST)
    patch_sum, patch_area = lax.psum((local_sum, local_area), ("bx", "by"))
    every_force = patch_sum / (1.0 + patch_area)
    start_own = lax.axis_index(("bx", "by")) * P_DEV
    patch_force = lax.dynamic_slice_in_dim(every_force, start_own, P_DEV, 0)
    face_force = weighted_area * jnp.dot(table, every_force, precision=lax.Precision.HIGHEST)
    source = objective_grad.at[:, :, :, 0].add(
        force_weight[:, None, None] * face_force.reshape(rows_i, rows_j)[None]
    )
    current = adjoint_start
    for alpha in (0.5, 1.0):
        received = with_halo(current, (("bx", 1), ("by", 2)), 2)
        extended = flip_rims(received, 2, low_flag, high_flag)
        residual = operate(extended, spectral_radius, flux_jacobian) + source
        current = adjoint_start - alpha * local_step * residual
    return (current, patch_force)


def solution(mesh):
    in_specs = (
        P(None, "bx", "by", None),
        P(None, "bx", "by", None),
        P(None, "bx", "by", None),
        P("bx", "by", None),
        P(),
        P("bx", None),
        P("bx", "by"),
        P("bx", "by"),
        P("bx", "by"),
        P(),
    )
    out_specs = (P(None, "bx", "by", None), P(("bx", "by")))
    return jax.shard_map(local, mesh=mesh, in_specs=in_specs, out_specs=out_specs, check_vma=False)
```

profile of v0, /device:TPU:20, one launch (start us, length us, event | category | flops | bytes accessed | tf_op | source)
XLA Modules:
  0.0 121.9 jit_solution(15572860991248611127)
XLA Ops:
  0.6 1.7 %copy.43 = f32[6,16,16,128]{3,0,2,1:T(8,128)S(1)} copy(f32[6,16,16,128]{3,2,1,0:T(8,128)} %param.12) | data formatting | bytes 1572864 | tf_op args[0]
  3.4 2.1 %collective-permute-start = (f32[6,2,16,128]{3,0,2,1:T(8,128)S(1)}, f32[6,2,16,128]{3,0,2,1:T(8,128)S(1)}, u32[]{:S(2)}, u32[]{:S(2)}) collective-permute-start(f32[6,2,16,128]{3,0,2,1:T(8,128)S(1)} %get-tuple-element.33), channel_id=1, source_target_pairs={{0,4},{4,8},{8,12},{12,16},{16,20},{20,24},{24,28},{1,5},{5,9},{9,... | collective-permute-start | bytes 294920 | tf_op jit(solution)/shard_map/ppermute | solution.py:19
  5.4 4.5 %collective-permute-start.1 = (f32[6,2,16,128]{3,0,2,1:T(8,128)S(1)}, f32[6,2,16,128]{3,0,2,1:T(8,128)S(1)}, u32[]{:S(2)}, u32[]{:S(2)}) collective-permute-start(f32[6,2,16,128]{3,0,2,1:T(8,128)S(1)} %get-tuple-element.32), channel_id=1, source_target_pairs={{4,0},{8,4},{12,8},{16,12},{20,16},{24,20},{28,24},{5,1},{9,5},{13... | collective-permute-start | bytes 294920 | tf_op jit(solution)/shard_map/ppermute | solution.py:20
  14.0 40.1 %all-reduce.2 = (f32[128]{0:T(128)S(1)}, f32[128]{0:T(128)S(1)}) all-reduce(f32[128]{0:T(128)S(1)} %convolution_bitcast_fusion.1, f32[128]{0:T(128)S(1)} %convolution_bitcast_fusion), channel_id=1, replica_groups=mesh['bx'=8,'by'=4] {'bx','by'}, use_global_device_ids=true, to_apply=%region_0.0 | all-reduce | flops 256 | bytes 2048 | tf_op jit(solution)/shard_map/psum | solution.py:95
  57.6 3.6 %scatter-add.4 = f32[6,16,16,128]{3,0,2,1:T(8,128)S(1)} dynamic-update-slice(f32[6,16,16,128]{3,0,2,1:T(8,128)S(1)} %copy.38, f32[6,16,16,1]{3,0,2,1:T(8,128)S(1)} %slice_add_fusion.1, s32[]{:T(128)} %constant.55.clone.1, s32[]{:T(128)} %constant.55.clone.1, s32[]{:T(128)} %constant.55.clone.1, s32[]{:T(128)} %constant.55.clone.1) | dynamic-update-slice | bytes 12292 | tf_op jit(solution)/shard_map/scatter-add | solution.py:100
  61.8 2.5 %collective-permute-start.3 = (f32[6,20,2,128]{3,0,2,1:T(8,128)S(1)}, f32[6,20,2,128]{3,0,2,1:T(8,128)S(1)}, u32[]{:S(2)}, u32[]{:S(2)}) collective-permute-start(f32[6,20,2,128]{3,0,2,1:T(8,128)S(1)} %get-tuple-element.29), channel_id=1, source_target_pairs={{1,0},{2,1},{3,2},{5,4},{6,5},{7,6},{9,8},{10,9},{11,10},{13,12},{... | collective-permute-start | bytes 368648 | tf_op jit(solution)/shard_map/ppermute | solution.py:20
  64.3 3.3 %collective-permute-start.2 = (f32[6,20,2,128]{3,0,2,1:T(8,128)S(1)}, f32[6,20,2,128]{3,0,2,1:T(8,128)S(1)}, u32[]{:S(2)}, u32[]{:S(2)}) collective-permute-start(f32[6,20,2,128]{3,0,2,1:T(8,128)S(1)} %get-tuple-element.28), channel_id=1, source_target_pairs={{0,1},{1,2},{2,3},{4,5},{5,6},{6,7},{8,9},{9,10},{10,11},{12,13},{... | collective-permute-start | bytes 368648 | tf_op jit(solution)/shard_map/ppermute | solution.py:19
  69.0 2.6 %collective-permute-done.2 = f32[6,20,2,128]{3,0,2,1:T(8,128)S(1)} collective-permute-done((f32[6,20,2,128]{3,0,2,1:T(8,128)S(1)}, f32[6,20,2,128]{3,0,2,1:T(8,128)S(1)}, u32[]{:S(2)}, u32[]{:S(2)}) %collective-permute-start.2) | collective-permute-done | bytes 122912 | tf_op jit(solution)/shard_map/ppermute | solution.py:19
  73.9 3.7 %fusion.25 = f32[6,16,16,128]{3,0,2,1:T(8,128)S(1)} fusion(f32[6,16,20,128]{3,0,2,1:T(8,128)S(1)} %slice.256, f32[6,2,20,128]{3,0,2,1:T(8,128)S(1)} %get-tuple-element.39, f32[6,2,20,128]{3,0,2,1:T(8,128)S(1)} %get-tuple-element.40, f32[16,16,128]{2,1,0:T(8,128)} %get-tuple-element.35, f32[6,16,16,128]{3,2,1,0:T(8,128)S(1)} %copy-done, ...), kind=kOutput, calls=%fused_computation.55 | convolution fusion | flops 17694720 | bytes 4984832 | tf_op jit(solution)/shard_map/fg,fxyz->gxyz/dot_general | solution.py:35
  77.7 2.5 %fusion.22 = f32[6,16,16,128]{3,0,2,1:T(8,128)S(1)} fusion(f32[6,16,16,128]{3,0,2,1:T(8,128)S(1)} %fusion.25, f32[6,20,16,128]{3,0,2,1:T(8,128)S(1)} %copy-done.2, f32[6,20,2,128]{3,0,2,1:T(8,128)S(1)} %copy-done.9, f32[6,20,2,128]{3,0,2,1:T(8,128)S(1)} %copy-done.7, f32[16,16,128]{2,1,0:T(8,128)S(1)} %copy-done.14, f32[6,16,16,128]{3,2,1,0:T(8,128)S(1)} %copy-done, ...), kind=kOutput, calls=%fused_computation.51 | convolution fusion | flops 17891328 | bytes 6033408 | tf_op jit(solution)/shard_map/fg,fxyz->gxyz/dot_general | solution.py:35
  80.2 2.5 %fusion.26 = f32[6,16,16,128]{3,0,2,1:T(8,128)S(1)} fusion(f32[6,16,16,128]{3,0,2,1:T(8,128)S(1)} %copy-done.4, f32[6,16,16,128]{3,0,2,1:T(8,128)S(1)} %scatter-add.4, f32[6,16,16,128]{3,0,2,1:T(8,128)S(1)} %fusion.22, f32[16,16,128]{2,1,0:T(8,128)S(1)} %copy-done.12, f32[16,16,128]{2,1,0:T(8,128)S(1)} %copy-done.17, f32[3,6,6]{2,1,0:T(8,128)S(1)} %copy-done.20), kind=kOutput, calls=%fused_computation.56 | convolution fusion | flops 17301504 | bytes 5246976 | tf_op jit(solution)/shard_map/fg,fxyz->gxyz/dot_general | solution.py:35
  82.8 1.9 %collective-permute-start.5 = (f32[6,2,16,128]{3,0,2,1:T(8,128)S(1)}, f32[6,2,16,128]{3,0,2,1:T(8,128)S(1)}, u32[]{:S(2)}, u32[]{:S(2)}) collective-permute-start(f32[6,2,16,128]{3,0,2,1:T(8,128)S(1)} %get-tuple-element.31), channel_id=1, source_target_pairs={{4,0},{8,4},{12,8},{16,12},{20,16},{24,20},{28,24},{5,1},{9,5},{13... | collective-permute-start | bytes 294920 | tf_op jit(solution)/shard_map/ppermute | solution.py:20
  84.7 2.4 %collective-permute-start.4 = (f32[6,2,16,128]{3,0,2,1:T(8,128)S(1)}, f32[6,2,16,128]{3,0,2,1:T(8,128)S(1)}, u32[]{:S(2)}, u32[]{:S(2)}) collective-permute-start(f32[6,2,16,128]{3,0,2,1:T(8,128)S(1)} %get-tuple-element.30), channel_id=1, source_target_pairs={{0,4},{4,8},{8,12},{12,16},{16,20},{20,24},{24,28},{1,5},{5,9},{9,... | collective-permute-start | bytes 294920 | tf_op jit(solution)/shard_map/ppermute | solution.py:19
  87.2 4.7 %collective-permute-done.4 = f32[6,2,16,128]{3,0,2,1:T(8,128)S(1)} collective-permute-done((f32[6,2,16,128]{3,0,2,1:T(8,128)S(1)}, f32[6,2,16,128]{3,0,2,1:T(8,128)S(1)}, u32[]{:S(2)}, u32[]{:S(2)}) %collective-permute-start.4) | collective-permute-done | bytes 98336 | tf_op jit(solution)/shard_map/ppermute | solution.py:19
  92.6 2.4 %collective-permute-start.7 = (f32[6,20,2,128]{3,0,2,1:T(8,128)}, f32[6,20,2,128]{3,0,2,1:T(8,128)S(1)}, u32[]{:S(2)}, u32[]{:S(2)}) collective-permute-start(f32[6,20,2,128]{3,0,2,1:T(8,128)} %get-tuple-element.27), channel_id=1, source_target_pairs={{1,0},{2,1},{3,2},{5,4},{6,5},{7,6},{9,8},{10,9},{11,10},{13,12},{... | collective-permute-start | bytes 368648 | tf_op jit(solution)/shard_map/ppermute | solution.py:20
  95.0 3.6 %collective-permute-start.6 = (f32[6,20,2,128]{3,0,2,1:T(8,128)}, f32[6,20,2,128]{3,0,2,1:T(8,128)S(1)}, u32[]{:S(2)}, u32[]{:S(2)}) collective-permute-start(f32[6,20,2,128]{3,0,2,1:T(8,128)} %get-tuple-element.26), channel_id=1, source_target_pairs={{0,1},{1,2},{2,3},{4,5},{5,6},{6,7},{8,9},{9,10},{10,11},{12,13},{... | collective-permute-start | bytes 368648 | tf_op jit(solution)/shard_map/ppermute | solution.py:19
  100.0 2.4 %collective-permute-done.6 = f32[6,20,2,128]{3,0,2,1:T(8,128)S(1)} collective-permute-done((f32[6,20,2,128]{3,0,2,1:T(8,128)}, f32[6,20,2,128]{3,0,2,1:T(8,128)S(1)}, u32[]{:S(2)}, u32[]{:S(2)}) %collective-permute-start.6) | collective-permute-done | bytes 122912 | tf_op jit(solution)/shard_map/ppermute | solution.py:19
  102.6 1.2 slice.268
  104.5 1.7 %rev.16 = f32[6,2,20,128]{3,0,2,1:T(8,128)} reverse(f32[6,2,20,128]{3,0,2,1:T(8,128)} %get-tuple-element.21), dimensions={3} | reverse | bytes 245760 | tf_op jit(solution)/shard_map/jit(_flip)/rev | solution.py:29
  106.2 1.6 %broadcast_select_fusion = f32[6,2,20,128]{3,0,2,1:T(8,128)} fusion(f32[6,2,20,128]{3,0,2,1:T(8,128)} %rev.16, f32[6,2,20,128]{3,0,2,1:T(8,128)} %get-tuple-element.21, pred[]{:T(512)} %bitcast.2), kind=kLoop, calls=%fused_computation.124 | loop fusion | flops 30720 | bytes 368641 | tf_op jit(solution)/shard_map/jit(_where)/select_n | solution.py:29
  107.8 1.7 %rev.15 = f32[6,2,20,128]{3,0,2,1:T(8,128)} reverse(f32[6,2,20,128]{3,0,2,1:T(8,128)} %get-tuple-element.20), dimensions={3} | reverse | bytes 245760 | tf_op jit(solution)/shard_map/jit(_flip)/rev | solution.py:30
  110.5 5.3 %fusion.12 = f32[6,16,16,128]{3,0,2,1:T(8,128)S(1)} fusion(f32[6,16,20,128]{3,0,2,1:T(8,128)} %slice.268, f32[6,2,20,128]{3,0,2,1:T(8,128)} %broadcast_select_fusion, f32[6,2,20,128]{3,0,2,1:T(8,128)S(1)} %broadcast_select_fusion.2, f32[6,16,16,128]{3,0,2,1:T(8,128)S(1)} %fusion.26, f32[16,16,128]{2,1,0:T(8,128)} %get-tuple-element.35, ...), kind=kOutput, calls=%fused_computation.39 | convolution fusion | flops 17694720 | bytes 5246976 | tf_op jit(solution)/shard_map/fg,fxyz->gxyz/dot_general | solution.py:35
  116.7 1.5 %fusion.9 = f32[6,16,16,128]{3,0,2,1:T(8,128)S(1)} fusion(f32[6,16,16,128]{3,0,2,1:T(8,128)S(1)} %fusion.12, f32[6,20,18,128]{3,0,2,1:T(8,128)S(1)} %get-tuple-element.25, f32[6,20,18,128]{3,0,2,1:T(8,128)S(1)} %get-tuple-element.24, f32[6,16,16,128]{3,0,2,1:T(8,128)S(1)} %fusion.26, f32[16,16,128]{2,1,0:T(8,128)S(1)} %copy-done.15, ...), kind=kOutput, calls=%fused_computation.35 | convolution fusion | flops 16711680 | bytes 9310208 | tf_op jit(solution)/shard_map/fg,fxyz->gxyz/dot_general | solution.py:35
  118.2 2.7 %fusion.27 = f32[6,16,16,128]{3,0,2,1:T(8,128)S(1)} fusion(f32[6,16,16,128]{3,0,2,1:T(8,128)S(1)} %scatter-add.4, f32[6,16,16,128]{3,0,2,1:T(8,128)S(1)} %fusion.9, f32[6,16,16,128]{3,0,2,1:T(8,128)S(1)} %fusion.26, f32[16,16,128]{2,1,0:T(8,128)S(1)} %copy-done.13, f32[16,16,128]{2,1,0:T(8,128)S(1)} %copy-done.11, f32[6,16,16,128]{3,2,1,0:T(8,128)S(1)} %copy-done, ...), kind=kOutput, calls=%fused_computation.57 | convolution fusion | flops 17301504 | bytes 6033408 | tf_op jit(solution)/shard_map/fg,fxyz->gxyz/dot_general | solution.py:35
  (94 shorter events, 16.7 us)
Async XLA Ops:
  0.6 10.0 %copy-start.19 = (f32[16,16]{1,0:T(8,128)S(1)}, f32[16,16]{1,0:T(8,128)}, u32[]{:S(2)}) copy-start(f32[16,16]{1,0:T(8,128)} %param.20) | copy-start | bytes 3076
  0.6 10.8 %copy-start.5 = (f32[6,16,16,128]{3,2,1,0:T(8,128)S(1)}, f32[6,16,16,128]{3,2,1,0:T(8,128)}, u32[]{:S(2)}) copy-start(f32[6,16,16,128]{3,2,1,0:T(8,128)} %param.13) | copy-start | bytes 2359300
  3.3 8.6 %copy-start.18 = (s32[16,16]{1,0:T(8,128)S(1)}, s32[16,16]{1,0:T(8,128)}, u32[]{:S(2)}) copy-start(s32[16,16]{1,0:T(8,128)} %param.19) | copy-start | bytes 3076
  3.3 8.7 %copy-start = (f32[6,16,16,128]{3,2,1,0:T(8,128)S(1)}, f32[6,16,16,128]{3,2,1,0:T(8,128)}, u32[]{:S(2)}) copy-start(f32[6,16,16,128]{3,2,1,0:T(8,128)} %param.12) | copy-start | bytes 2359300
  3.3 9.4 %copy-start.21 = (f32[6]{0:T(128)S(1)}, f32[6]{0:T(128)}, u32[]{:S(2)}) copy-start(f32[6]{0:T(128)} %param.21) | copy-start | bytes 76
  3.4 57.9 %collective-permute-start = (f32[6,2,16,128]{3,0,2,1:T(8,128)S(1)}, f32[6,2,16,128]{3,0,2,1:T(8,128)S(1)}, u32[]{:S(2)}, u32[]{:S(2)}) collective-permute-start(f32[6,2,16,128]{3,0,2,1:T(8,128)S(1)} %get-tuple-element.33), channel_id=1, source_target_pairs={{0,4},{4,8},{8,12},{12,16},{16,20},{20,24},{24,28},{1,5},{5,9},{9,... | collective-permute-start | bytes 294920 | tf_op jit(solution)/shard_map/ppermute | solution.py:19
  5.4 56.3 %collective-permute-start.1 = (f32[6,2,16,128]{3,0,2,1:T(8,128)S(1)}, f32[6,2,16,128]{3,0,2,1:T(8,128)S(1)}, u32[]{:S(2)}, u32[]{:S(2)}) collective-permute-start(f32[6,2,16,128]{3,0,2,1:T(8,128)S(1)} %get-tuple-element.32), channel_id=1, source_target_pairs={{4,0},{8,4},{12,8},{16,12},{20,16},{24,20},{28,24},{5,1},{9,5},{13... | collective-permute-start | bytes 294920 | tf_op jit(solution)/shard_map/ppermute | solution.py:20
  11.4 43.2 %copy-start.16 = (f32[3,16,16,128]{3,2,1,0:T(8,128)S(1)}, f32[3,16,16,128]{3,2,1,0:T(8,128)}, u32[]{:S(2)}) copy-start(f32[3,16,16,128]{3,2,1,0:T(8,128)} %param.14) | copy-start | bytes 1179652
  61.2 6.5 %copy-start.10 = (f32[16,16,128]{2,1,0:T(8,128)S(1)}, f32[16,16,128]{2,1,0:T(8,128)}, u32[]{:S(2)}) copy-start(f32[16,16,128]{2,1,0:T(8,128)} %param.15) | copy-start | bytes 393220
  61.8 10.1 %copy-start.1 = (f32[6,20,16,128]{3,0,2,1:T(8,128)}, f32[6,20,16,128]{3,0,2,1:T(8,128)S(1)}, u32[]{:S(2)}) copy-start(f32[6,20,16,128]{3,0,2,1:T(8,128)S(1)} %constant_dynamic-update-slice_fusion) | copy-start | bytes 2949124
  61.8 7.2 %collective-permute-start.3 = (f32[6,20,2,128]{3,0,2,1:T(8,128)S(1)}, f32[6,20,2,128]{3,0,2,1:T(8,128)S(1)}, u32[]{:S(2)}, u32[]{:S(2)}) collective-permute-start(f32[6,20,2,128]{3,0,2,1:T(8,128)S(1)} %get-tuple-element.29), channel_id=1, source_target_pairs={{1,0},{2,1},{3,2},{5,4},{6,5},{7,6},{9,8},{10,9},{11,10},{13,12},{... | collective-permute-start | bytes 368648 | tf_op jit(solution)/shard_map/ppermute | solution.py:20
  64.3 7.2 %collective-permute-start.2 = (f32[6,20,2,128]{3,0,2,1:T(8,128)S(1)}, f32[6,20,2,128]{3,0,2,1:T(8,128)S(1)}, u32[]{:S(2)}, u32[]{:S(2)}) collective-permute-start(f32[6,20,2,128]{3,0,2,1:T(8,128)S(1)} %get-tuple-element.28), channel_id=1, source_target_pairs={{0,1},{1,2},{2,3},{4,5},{5,6},{6,7},{8,9},{9,10},{10,11},{12,13},{... | collective-permute-start | bytes 368648 | tf_op jit(solution)/shard_map/ppermute | solution.py:19
  69.0 2.8 %copy-start.6 = (f32[6,20,2,128]{3,0,2,1:T(8,128)}, f32[6,20,2,128]{3,0,2,1:T(8,128)S(1)}, u32[]{:S(2)}) copy-start(f32[6,20,2,128]{3,0,2,1:T(8,128)S(1)} %collective-permute-done.3) | copy-start | bytes 368644
  73.9 3.7 %copy-start.2 = (f32[6,20,16,128]{3,0,2,1:T(8,128)S(1)}, f32[6,20,16,128]{3,0,2,1:T(8,128)}, u32[]{:S(2)}) copy-start(f32[6,20,16,128]{3,0,2,1:T(8,128)} %copy-done.1) | copy-start | bytes 2949124
  73.9 3.7 %copy-start.7 = (f32[6,20,2,128]{3,0,2,1:T(8,128)S(1)}, f32[6,20,2,128]{3,0,2,1:T(8,128)}, u32[]{:S(2)}) copy-start(f32[6,20,2,128]{3,0,2,1:T(8,128)} %copy-done.6) | copy-start | bytes 368644
  73.9 3.7 %copy-start.9 = (f32[6,20,2,128]{3,0,2,1:T(8,128)S(1)}, f32[6,20,2,128]{3,0,2,1:T(8,128)}, u32[]{:S(2)}) copy-start(f32[6,20,2,128]{3,0,2,1:T(8,128)} %copy-done.8) | copy-start | bytes 368644
  73.9 3.7 %copy-start.14 = (f32[16,16,128]{2,1,0:T(8,128)S(1)}, f32[16,16,128]{2,1,0:T(8,128)}, u32[]{:S(2)}) copy-start(f32[16,16,128]{2,1,0:T(8,128)} %get-tuple-element.36) | copy-start | bytes 393220
  77.7 2.5 %copy-start.4 = (f32[6,16,16,128]{3,0,2,1:T(8,128)S(1)}, f32[6,16,16,128]{3,0,2,1:T(8,128)}, u32[]{:S(2)}) copy-start(f32[6,16,16,128]{3,0,2,1:T(8,128)} %copy-done.3) | copy-start | bytes 2359300
  77.7 2.5 %copy-start.12 = (f32[16,16,128]{2,1,0:T(8,128)S(1)}, f32[16,16,128]{2,1,0:T(8,128)}, u32[]{:S(2)}) copy-start(f32[16,16,128]{2,1,0:T(8,128)} %get-tuple-element.34) | copy-start | bytes 393220
  82.7 15.9 %copy-start.24 = (f32[128]{0:T(128)S(1)}, f32[128]{0:T(128)}, u32[]{:S(2)}) copy-start(f32[128]{0:T(128)} %copy-done.23) | copy-start | bytes 1540
  82.8 4.4 %collective-permute-start.5 = (f32[6,2,16,128]{3,0,2,1:T(8,128)S(1)}, f32[6,2,16,128]{3,0,2,1:T(8,128)S(1)}, u32[]{:S(2)}, u32[]{:S(2)}) collective-permute-start(f32[6,2,16,128]{3,0,2,1:T(8,128)S(1)} %get-tuple-element.31), channel_id=1, source_target_pairs={{4,0},{8,4},{12,8},{16,12},{20,16},{24,20},{28,24},{5,1},{9,5},{13... | collective-permute-start | bytes 294920 | tf_op jit(solution)/shard_map/ppermute | solution.py:20
  84.7 7.2 %collective-permute-start.4 = (f32[6,2,16,128]{3,0,2,1:T(8,128)S(1)}, f32[6,2,16,128]{3,0,2,1:T(8,128)S(1)}, u32[]{:S(2)}, u32[]{:S(2)}) collective-permute-start(f32[6,2,16,128]{3,0,2,1:T(8,128)S(1)} %get-tuple-element.30), channel_id=1, source_target_pairs={{0,4},{4,8},{8,12},{12,16},{16,20},{20,24},{24,28},{1,5},{5,9},{9,... | collective-permute-start | bytes 294920 | tf_op jit(solution)/shard_map/ppermute | solution.py:19
  92.6 7.4 %collective-permute-start.7 = (f32[6,20,2,128]{3,0,2,1:T(8,128)}, f32[6,20,2,128]{3,0,2,1:T(8,128)S(1)}, u32[]{:S(2)}, u32[]{:S(2)}) collective-permute-start(f32[6,20,2,128]{3,0,2,1:T(8,128)} %get-tuple-element.27), channel_id=1, source_target_pairs={{1,0},{2,1},{3,2},{5,4},{6,5},{7,6},{9,8},{10,9},{11,10},{13,12},{... | collective-permute-start | bytes 368648 | tf_op jit(solution)/shard_map/ppermute | solution.py:20
  95.0 7.4 %collective-permute-start.6 = (f32[6,20,2,128]{3,0,2,1:T(8,128)}, f32[6,20,2,128]{3,0,2,1:T(8,128)S(1)}, u32[]{:S(2)}, u32[]{:S(2)}) collective-permute-start(f32[6,20,2,128]{3,0,2,1:T(8,128)} %get-tuple-element.26), channel_id=1, source_target_pairs={{0,1},{1,2},{2,3},{4,5},{5,6},{6,7},{8,9},{9,10},{10,11},{12,13},{... | collective-permute-start | bytes 368648 | tf_op jit(solution)/shard_map/ppermute | solution.py:19
  (9 other events, 11.8 us)
where the time goes:
time: 123 us; the launch traced here: 122 us
  blocking collectives  40.1 us (33%)
  starting transfers between devices  22.8 us (19%)
  matrix products  19.6 us (16%)
  local copies, waits for them, and re-layouts  19.4 us (16%)
  waiting for transfers between devices  11.2 us (9%)
  other arithmetic  5.71 us (5%)
  between operations  3.11 us (3%)
    psum x1, blocking collectives, local(): patch_sum, patch_area = lax.psum((local_sum, local_area), ('bx', 'by'))  40.1 us
    dot_general x6, matrix products, transpose_apply(): jnp.einsum('fg,fxyz->gxyz', matrix, field, precision=lax.Precision.HIGHEST)  18.2 us
    ppermute x4, starting transfers between devices, with_halo(): after = lax.ppermute(first, axis, down)  11.4 us
    ppermute x4, starting transfers between devices, with_halo(): before = lax.ppermute(last, axis, up)  11.4 us
    ppermute x4, waiting for transfers between devices, with_halo(): before = lax.ppermute(last, axis, up)  9.68 us
    unnamed x56, local copies, waits for them, and re-layouts  6.57 us
    scatter-add x1, local copies, waits for them, and re-layouts, local(): objective_grad.at[:, :, :, 0]  3.57 us
    rev x2, local copies, waits for them, and re-layouts, flip_rims(): lower = jnp.where(low_flag == 1, jnp.flip(lower, 3), lower)  2.47 us
  transfers between devices with their start and end apart: 8, of which 6 were waited for; matrix products, arithmetic and copies ran while one was open for 9% of the time, Pallas kernels for 0%

commit v1 on v0

v1 whole, which is shorter than its diff:
```python
import functools

import jax
import jax.numpy as jnp
from jax import lax
from jax.experimental import pallas as pl
from jax.experimental.pallas import tpu as pltpu
from jax.sharding import PartitionSpec as P

P_DEV = 4
EPS = 0.1
FIELDS = 6
MESH = pl.DeviceIdType.MESH


def smooth_kernel(
    nx, ny, rows_i, rows_j,
    adj_hbm, obj_hbm, rad_hbm, step_hbm, patch_ref, area_ref, jac_ref, orient_ref, count_ref, weight_ref,
    out_ref, force_ref,
    adj, one, obj, rad, step, wall, pack1, pack2, halo1, halo2, turned, mine1, mine2, got1, got2,
    load_sem, hsend1, hrecv1, hsend2, hrecv2, psend1, precv1, psend2, precv2,
):
    cells = rows_i * rows_j
    pad = 2 * rows_j
    lanes = adj.shape[2]
    at_x = lax.axis_index("bx")
    at_y = lax.axis_index("by")
    patch_total = P_DEV * nx * ny
    groups = -(-patch_total // lanes)

    loads = [
        pltpu.make_async_copy(adj_hbm, adj.at[:, pl.ds(pad, cells), :], load_sem.at[0]),
        pltpu.make_async_copy(obj_hbm, obj, load_sem.at[1]),
        pltpu.make_async_copy(rad_hbm, rad, load_sem.at[2]),
        pltpu.make_async_copy(step_hbm, step, load_sem.at[3]),
    ]
    for copy in loads:
        copy.start()

    barrier = pltpu.get_barrier_semaphore()
    for o in range(1, nx):
        pl.semaphore_signal(barrier, inc=1, device_id=(lax.rem(at_x + o, nx), at_y), device_id_type=MESH)
    for o in range(1, ny):
        pl.semaphore_signal(barrier, inc=1, device_id=(at_x, lax.rem(at_y + o, ny)), device_id_type=MESH)

    zero = jnp.zeros((pad, lanes), jnp.float32)
    for ref in (adj, one):
        for f in range(FIELDS):
            ref[f, pl.ds(0, pad), :] = zero
            ref[f, pl.ds(pad + cells, pad), :] = zero
    pl.semaphore_wait(barrier, nx + ny - 2)

    has = [at_x > 0, at_x < nx - 1, at_y > 0, at_y < ny - 1]
    source_has = [has[1], has[0], has[3], has[2]]
    targets = [
        (lax.min(at_x + 1, nx - 1), at_y),
        (lax.max(at_x - 1, 0), at_y),
        (at_x, lax.min(at_y + 1, ny - 1)),
        (at_x, lax.max(at_y - 1, 0)),
    ]

    def halo_copies(low_rows, high_rows, pack, halo, send_sem, recv_sem):
        sources = [high_rows, low_rows, pack.at[1], pack.at[0]]
        return [
            pltpu.make_async_remote_copy(
                src_ref=sources[s], dst_ref=halo.at[s], send_sem=send_sem.at[s], recv_sem=recv_sem.at[s],
                device_id=targets[s], device_id_type=MESH,
            )
            for s in range(4)
        ]

    def start(copies, s):
        @pl.when(source_has[s])
        def _():
            copies[s].start()

    def pack_faces(ref, pack):
        for side, first in ((0, 0), (1, rows_j - 2)):
            for f in range(FIELDS):
                for layer in range(2):
                    pack[side, f, pl.ds(layer * rows_i, rows_i), :] = ref[
                        f, pl.ds(pad + first + layer, rows_i, stride=rows_j), :
                    ]

    first_copies = halo_copies(
        adj_hbm.at[:, pl.ds(0, pad), :], adj_hbm.at[:, pl.ds(cells - pad, pad), :], pack1, halo1, hsend1, hrecv1
    )
    start(first_copies, 0)
    start(first_copies, 1)
    loads[0].wait()
    pack_faces(adj, pack1)
    start(first_copies, 2)
    start(first_copies, 3)

    weights = [weight_ref[f] for f in range(FIELDS)]
    patch_t = jnp.transpose(patch_ref[...])
    area_t = jnp.transpose(area_ref[...])
    spot = lax.broadcasted_iota(jnp.int32, (rows_j, rows_i), 1) * rows_j + lax.broadcasted_iota(
        jnp.int32, (rows_j, rows_i), 0
    )
    area_t = jnp.where(spot < count_ref[0, 0], area_t, 0.0)
    lane = lax.broadcasted_iota(jnp.int32, (rows_j, lanes), 1)
    second = lax.broadcasted_iota(jnp.int32, (rows_j, lanes), 0)
    sums = [jnp.zeros((rows_j, lanes), jnp.float32) for _ in range(groups)]
    areas = [jnp.zeros((rows_j, lanes), jnp.float32) for _ in range(groups)]
    for i in range(rows_i):
        weighted = weights[0] * adj[0, pl.ds(pad + i * rows_j, rows_j), :]
        for f in range(1, FIELDS):
            weighted = weighted + weights[f] * adj[f, pl.ds(pad + i * rows_j, rows_j), :]
        area = area_t[:, i : i + 1]
        value = area * weighted[:, 0:1]
        patch = patch_t[:, i : i + 1]
        for r in range(groups):
            hit = patch == lane + r * lanes
            sums[r] = sums[r] + jnp.where(hit, value, 0.0)
            areas[r] = areas[r] + jnp.where(hit, area, 0.0)
    for r in range(groups):
        mine1[pl.ds(r, 1), :] = jnp.sum(sums[r], axis=0, keepdims=True)
        mine1[pl.ds(groups + r, 1), :] = jnp.sum(areas[r], axis=0, keepdims=True)

    x_copies = [
        pltpu.make_async_remote_copy(
            src_ref=mine1, dst_ref=got1.at[o - 1], send_sem=psend1.at[o - 1], recv_sem=precv1.at[o - 1],
            device_id=(lax.rem(at_x + o, nx), at_y), device_id_type=MESH,
        )
        for o in range(1, nx)
    ]
    y_copies = [
        pltpu.make_async_remote_copy(
            src_ref=mine2, dst_ref=got2.at[o - 1], send_sem=psend2.at[o - 1], recv_sem=precv2.at[o - 1],
            device_id=(at_x, lax.rem(at_y + o, ny)), device_id_type=MESH,
        )
        for o in range(1, ny)
    ]
    for copy in x_copies:
        copy.start()

    scale = 0.5 / EPS

    def coupled(direction, g, fields):
        total = (jac_ref[direction, 0, g] * scale) * fields[0]
        for f in range(1, FIELDS):
            total = total + (jac_ref[direction, f, g] * scale) * fields[f]
        return total

    def section(ref, target, offset, factor, with_wall, first_i, last_i):
        def body(i, carry):
            base = pl.multiple_of(i * rows_j, rows_j)

            def rows(f, shift):
                return ref[f, pl.ds(base + (pad + shift), rows_j), :]

            center = [rows(f, 0) for f in range(FIELDS)]
            six = [6.0 * c for c in center]
            total = [None] * FIELDS
            for direction in range(3):
                near, far = [], []
                for f in range(FIELDS):
                    if direction == 0:
                        f1, b1, f2, b2 = (rows(f, s * rows_j) for s in (1, -1, 2, -2))
                    elif direction == 1:
                        f1 = jnp.where(second < rows_j - 1, rows(f, 1), 0.0)
                        b1 = jnp.where(second >= 1, rows(f, -1), 0.0)
                        f2 = jnp.where(second < rows_j - 2, rows(f, 2), 0.0)
                        b2 = jnp.where(second >= 2, rows(f, -2), 0.0)
                    else:
                        c = center[f]
                        f1 = jnp.where(lane < lanes - 1, pltpu.roll(c, lanes - 1, 1), 0.0)
                        b1 = jnp.where(lane >= 1, pltpu.roll(c, 1, 1), 0.0)
                        f2 = jnp.where(lane < lanes - 2, pltpu.roll(c, lanes - 2, 1), 0.0)
                        b2 = jnp.where(lane >= 2, pltpu.roll(c, 2, 1), 0.0)
                    both = f1 + b1
                    near.append(both if direction == 2 else f1 - b1)
                    far.append((f2 + b2) - 4.0 * both + six[f])
                radius = EPS * rad[direction, pl.ds(base, rows_j), :]
                for g in range(FIELDS):
                    term = radius * (far[g] + coupled(direction, g, near))
                    total[g] = term if direction == 0 else total[g] + term
            size = step[pl.ds(base, rows_j), :]
            if factor != 1.0:
                size = factor * size
            at_wall = wall[pl.ds(base, rows_j), :] if with_wall else None
            for g in range(FIELDS):
                whole = total[g] + obj[g, pl.ds(base, rows_j), :]
                if with_wall:
                    whole = whole + weights[g] * at_wall
                start_value = center[g] if ref is adj else adj[g, pl.ds(base + pad, rows_j), :]
                target[g, pl.ds(base + offset, rows_j), :] = start_value - size * whole
            return carry

        lax.fori_loop(first_i, last_i, body, 0)

    def turn(halo, side, flag):
        row = lax.broadcasted_iota(jnp.int32, (lanes, lanes), 0)
        col = lax.broadcasted_iota(jnp.int32, (lanes, lanes), 1)
        goal = jnp.where(flag == 1, lanes - 1 - col, col)
        matrix = jnp.where(row == goal, 1.0, 0.0).astype(jnp.float32)
        values = halo[side].reshape(FIELDS * pad, lanes)
        moved = jnp.dot(values, matrix, precision=lax.Precision.HIGHEST, preferred_element_type=jnp.float32)
        turned[...] = moved.reshape(FIELDS, pad, lanes)

    def correct(halo, side, target, offset, factor):
        direction, high = side // 2, side % 2
        count = rows_j if direction == 0 else rows_i
        layers = rows_i if direction == 0 else rows_j
        near_at, far_at = (0, count) if high else (count, 0)
        edge, inner = (layers - 1, layers - 2) if high else (0, 1)

        def at(layer, extra):
            if direction == 0:
                return pl.ds(extra + layer * rows_j, rows_j)
            return pl.ds(extra + layer, rows_i, stride=rows_j)

        def load(f, first):
            if direction == 0:
                return turned[f, pl.ds(first, count), :]
            return halo[side, f, pl.ds(first, count), :]

        near = [load(f, near_at) for f in range(FIELDS)]
        size_edge = (factor * EPS) * step[at(edge, 0), :] * rad[direction, at(edge, 0), :]
        size_inner = (factor * EPS) * step[at(inner, 0), :] * rad[direction, at(inner, 0), :]
        for g in range(FIELDS):
            mixed = coupled(direction, g, near)
            if not high:
                mixed = -mixed
            change = mixed + (load(g, far_at) - 4.0 * near[g])
            target[g, at(edge, offset), :] = target[g, at(edge, offset), :] - size_edge * change
            target[g, at(inner, offset), :] = target[g, at(inner, offset), :] - size_inner * near[g]

    def finish_halo(copies, halo, target, offset, factor):
        for s in range(4):
            @pl.when(has[s])
            def _(s=s):
                copies[s].wait_recv()
                if s < 2:
                    turn(halo, s, orient_ref[0, s])
                correct(halo, s, target, offset, factor)

    for copy in loads[1:]:
        copy.wait()
    half = rows_i // 2
    section(adj, one, pad, 0.5, False, 0, half)
    for copy in x_copies:
        copy.wait_recv()
    mine2[...] = functools.reduce(lambda a, b: a + b, [got1[o] for o in range(nx - 1)], mine1[...])
    for copy in y_copies:
        copy.start()
    section(adj, one, pad, 0.5, False, half, rows_i)
    finish_halo(first_copies, halo1, one, pad, 0.5)
    for copy in y_copies:
        copy.wait_recv()
    summed = functools.reduce(lambda a, b: a + b, [got2[o] for o in range(ny - 1)], mine2[...])
    force = summed[:groups] / (1.0 + summed[groups:])

    for i in range(rows_i):
        patch = patch_t[:, i : i + 1]
        hits = jnp.where(patch == lane, force[0:1], 0.0)
        for r in range(1, groups):
            hits = hits + jnp.where(patch == lane + r * lanes, force[r : r + 1], 0.0)
        face = area_t[:, i : i + 1] * jnp.sum(hits, axis=1, keepdims=True)
        face = jnp.where(lane == 0, face, 0.0)
        wall[pl.ds(i * rows_j, rows_j), :] = face
        moved = 0.5 * step[pl.ds(i * rows_j, rows_j), :] * face
        for f in range(FIELDS):
            at = pl.ds(pad + i * rows_j, rows_j)
            one[f, at, :] = one[f, at, :] - weights[f] * moved

    second_copies = halo_copies(
        one.at[:, pl.ds(pad, pad), :], one.at[:, pl.ds(cells, pad), :], pack2, halo2, hsend2, hrecv2
    )
    start(second_copies, 0)
    start(second_copies, 1)
    pack_faces(one, pack2)
    start(second_copies, 2)
    start(second_copies, 3)

    own = (at_x * ny + at_y) * P_DEV
    place = lax.broadcasted_iota(jnp.int32, (groups, lanes), 0) * lanes + lax.broadcasted_iota(
        jnp.int32, (groups, lanes), 1
    )
    for q in range(P_DEV):
        force_ref[q] = jnp.sum(jnp.where(place == own + q, force, 0.0))

    section(one, out_ref, 0, 1.0, True, 0, rows_i)
    finish_halo(second_copies, halo2, out_ref, 0, 1.0)

    for copies in (first_copies, second_copies):
        for s in range(4):
            @pl.when(source_has[s])
            def _(s=s, copies=copies):
                copies[s].wait_send()
    for copy in x_copies + y_copies:
        copy.wait_send()


def local(
    adjoint_start,
    objective_grad,
    spectral_radius,
    local_step,
    flux_jacobian,
    face_orient,
    wall_count,
    face_patch,
    face_area,
    force_weight,
):
    fields, rows_i, rows_j, lanes = adjoint_start.shape
    cells, pad = rows_i * rows_j, 2 * rows_j
    nx, ny = lax.axis_size("bx"), lax.axis_size("by")
    groups = -(-P_DEV * nx * ny // lanes)
    f32 = jnp.float32
    vmem = pl.BlockSpec(memory_space=pltpu.VMEM)
    smem = pl.BlockSpec(memory_space=pltpu.SMEM)
    anywhere = pl.BlockSpec(memory_space=pl.ANY)
    dma = pltpu.SemaphoreType.DMA
    result, force = pl.pallas_call(
        functools.partial(smooth_kernel, nx, ny, rows_i, rows_j),
        out_shape=(
            jax.ShapeDtypeStruct((fields, cells, lanes), f32),
            jax.ShapeDtypeStruct((P_DEV,), f32),
        ),
        in_specs=[anywhere] * 4 + [vmem] * 2 + [smem] * 4,
        out_specs=(vmem, smem),
        scratch_shapes=[
            pltpu.VMEM((fields, cells + 2 * pad, lanes), f32),
            pltpu.VMEM((fields, cells + 2 * pad, lanes), f32),
            pltpu.VMEM((fields, cells, lanes), f32),
            pltpu.VMEM((3, cells, lanes), f32),
            pltpu.VMEM((cells, lanes), f32),
            pltpu.VMEM((cells, lanes), f32),
            pltpu.VMEM((2, fields, 2 * rows_i, lanes), f32),
            pltpu.VMEM((2, fields, 2 * rows_i, lanes), f32),
            pltpu.VMEM((4, fields, pad, lanes), f32),
            pltpu.VMEM((4, fields, pad, lanes), f32),
            pltpu.VMEM((fields, pad, lanes), f32),
            pltpu.VMEM((2 * groups, lanes), f32),
            pltpu.VMEM((2 * groups, lanes), f32),
            pltpu.VMEM((nx - 1, 2 * groups, lanes), f32),
            pltpu.VMEM((ny - 1, 2 * groups, lanes), f32),
            dma((4,)), dma((4,)), dma((4,)), dma((4,)), dma((4,)),
            dma((nx - 1,)), dma((nx - 1,)), dma((ny - 1,)), dma((ny - 1,)),
        ],
        compiler_params=pltpu.CompilerParams(
            collective_id=0, has_side_effects=True, vmem_limit_bytes=32 * 1024 * 1024
        ),
    )(
        adjoint_start.reshape(fields, cells, lanes),
        objective_grad.reshape(fields, cells, lanes),
        spectral_radius.reshape(3, cells, lanes),
        local_step.reshape(cells, lanes),
        face_patch,
        face_area,
        flux_jacobian,
        face_orient,
        wall_count,
        force_weight,
    )
    return result.reshape(adjoint_start.shape), force


def solution(mesh):
    in_specs = (
        P(None, "bx", "by", None),
        P(None, "bx", "by", None),
        P(None, "bx", "by", None),
        P("bx", "by", None),
        P(),
        P("bx", None),
        P("bx", "by"),
        P("bx", "by"),
        P("bx", "by"),
        P(),
    )
    out_specs = (P(None, "bx", "by", None), P(("bx", "by")))
    return jax.shard_map(local, mesh=mesh, in_specs=in_specs, out_specs=out_specs, check_vma=False)
```

time: 123 us -> 29.3 us (0.24)
  the two profiles are of different devices: /device:TPU:20 before, /device:TPU:0 now
where the time goes in v1:
time: 29.3 us; the launch traced here: 28.8 us
  Pallas kernels  19.8 us (68%)
  local copies, waits for them, and re-layouts  7.62 us (26%)
  between operations  1.33 us (5%)
    pallas_call x1, Pallas kernels, local(): pl.pallas_call(functools.partial(smooth_kernel, nx, ny, rows_i, rows_j),...  19.8 us
    unnamed x20, local copies, waits for them, and re-layouts  7.62 us

profile of v1, /device:TPU:0, one launch (start us, length us, event | category | flops | bytes accessed | tf_op | source)
XLA Modules:
  0.0 28.8 jit_solution(1949492546521843307)
XLA Ops:
  0.6 0.0 copy-start.5
  1.3 0.0 copy-start.7
  1.3 0.0 copy-start.8
  1.3 0.0 copy-done.5
  1.3 0.6 %copy-done.7 = s32[1,2]{1,0:T(1,128)S(1)} copy-done((s32[1,2]{1,0:T(1,128)S(1)}, s32[1,2]{1,0:T(1,128)}, u32[]{:S(2)}) %copy-start.7) | copy-done | bytes 32
  2.0 0.0 copy-done.8
  2.0 0.0 copy-start
  2.0 1.1 %copy-done = f32[6,16,16,128]{3,2,1,0:T(8,128)S(1)} copy-done((f32[6,16,16,128]{3,2,1,0:T(8,128)S(1)}, f32[6,16,16,128]{3,2,1,0:T(8,128)}, u32[]{:S(2)}) %copy-start) | copy-done | bytes 786456
  3.1 0.0 copy-start.1
  3.1 1.1 %copy-done.1 = f32[6,16,16,128]{3,2,1,0:T(8,128)S(1)} copy-done((f32[6,16,16,128]{3,2,1,0:T(8,128)S(1)}, f32[6,16,16,128]{3,2,1,0:T(8,128)}, u32[]{:S(2)}) %copy-start.1) | copy-done | bytes 786456
  4.2 0.0 copy-start.2
  4.2 1.0 %copy-done.2 = f32[3,16,16,128]{3,2,1,0:T(8,128)S(1)} copy-done((f32[3,16,16,128]{3,2,1,0:T(8,128)S(1)}, f32[3,16,16,128]{3,2,1,0:T(8,128)}, u32[]{:S(2)}) %copy-start.2) | copy-done | bytes 393240
  5.2 0.0 copy-start.3
  5.2 0.9 %copy-done.3 = f32[16,16,128]{2,1,0:T(8,128)S(1)} copy-done((f32[16,16,128]{2,1,0:T(8,128)S(1)}, f32[16,16,128]{2,1,0:T(8,128)}, u32[]{:S(2)}) %copy-start.3) | copy-done | bytes 131096
  6.1 0.0 copy-start.4
  6.1 0.7 %copy-done.4 = f32[3,6,6]{2,1,0:T(8,128)S(1)} copy-done((f32[3,6,6]{2,1,0:T(8,128)S(1)}, f32[3,6,6]{2,1,0:T(8,128)}, u32[]{:S(2)}) %copy-start.4) | copy-done | bytes 456
  6.9 0.0 copy-start.6
  6.9 0.7 %copy-done.6 = f32[16,16]{1,0:T(8,128)S(1)} copy-done((f32[16,16]{1,0:T(8,128)S(1)}, f32[16,16]{1,0:T(8,128)}, u32[]{:S(2)}) %copy-start.6) | copy-done | bytes 1048
  7.5 19.8 %shard_map.113 = (f32[6,256,128]{2,1,0:T(8,128)S(1)}, f32[4]{0:T(128)S(1)}) custom-call(f32[6,256,128]{2,1,0:T(8,128)S(1)} %bitcast.5, f32[6,256,128]{2,1,0:T(8,128)S(1)} %bitcast.6, f32[3,256,128]{2,1,0:T(8,128)S(1)} %bitcast.8, f32[256,128]{1,0:T(8,128)S(1)} %bitcast.9, s32[16,16]{1,0:T(8,128)S(1)} %copy-done.5, f32[16,16]{1,0:T(8,128)S(1)} %copy-done.6, ...), custom_call_target="tpu_custom_call" | custom-call | tf_op jit(solution)/shard_map/pallas_call | solution.py:317
  27.4 0.9 %copy.15 = f32[6,16,16,128]{3,2,1,0:T(8,128)} copy(f32[6,16,16,128]{3,2,1,0:T(8,128)S(1)} %bitcast.7) | data formatting | bytes 1572864
  28.2 0.5 %copy.16 = f32[4]{0:T(128)} copy(f32[4]{0:T(128)S(1)} %get-tuple-element.9) | data formatting | bytes 32
Async XLA Ops:
  0.6 0.7 %copy-start.5 = (s32[16,16]{1,0:T(8,128)S(1)}, s32[16,16]{1,0:T(8,128)}, u32[]{:S(2)}) copy-start(s32[16,16]{1,0:T(8,128)} %patch_ref.1) | copy-start | bytes 3076
  1.3 0.7 %copy-start.7 = (s32[1,2]{1,0:T(1,128)S(1)}, s32[1,2]{1,0:T(1,128)}, u32[]{:S(2)}) copy-start(s32[1,2]{1,0:T(1,128)} %orient_ref.1) | copy-start | bytes 28
  1.3 0.7 %copy-start.8 = (f32[6]{0:T(128)S(1)}, f32[6]{0:T(128)}, u32[]{:S(2)}) copy-start(f32[6]{0:T(128)} %weight_ref.1) | copy-start | bytes 76
  2.0 1.1 %copy-start = (f32[6,16,16,128]{3,2,1,0:T(8,128)S(1)}, f32[6,16,16,128]{3,2,1,0:T(8,128)}, u32[]{:S(2)}) copy-start(f32[6,16,16,128]{3,2,1,0:T(8,128)} %param.10) | copy-start | bytes 2359300
  3.1 1.1 %copy-start.1 = (f32[6,16,16,128]{3,2,1,0:T(8,128)S(1)}, f32[6,16,16,128]{3,2,1,0:T(8,128)}, u32[]{:S(2)}) copy-start(f32[6,16,16,128]{3,2,1,0:T(8,128)} %param.11) | copy-start | bytes 2359300
  4.2 1.0 %copy-start.2 = (f32[3,16,16,128]{3,2,1,0:T(8,128)S(1)}, f32[3,16,16,128]{3,2,1,0:T(8,128)}, u32[]{:S(2)}) copy-start(f32[3,16,16,128]{3,2,1,0:T(8,128)} %param.12) | copy-start | bytes 1179652
  5.2 0.9 %copy-start.3 = (f32[16,16,128]{2,1,0:T(8,128)S(1)}, f32[16,16,128]{2,1,0:T(8,128)}, u32[]{:S(2)}) copy-start(f32[16,16,128]{2,1,0:T(8,128)} %param.13) | copy-start | bytes 393220
  6.1 0.7 %copy-start.4 = (f32[3,6,6]{2,1,0:T(8,128)S(1)}, f32[3,6,6]{2,1,0:T(8,128)}, u32[]{:S(2)}) copy-start(f32[3,6,6]{2,1,0:T(8,128)} %jac_ref.1) | copy-start | bytes 1300
  6.9 0.7 %copy-start.6 = (f32[16,16]{1,0:T(8,128)S(1)}, f32[16,16]{1,0:T(8,128)}, u32[]{:S(2)}) copy-start(f32[16,16]{1,0:T(8,128)} %area_ref.1) | copy-start | bytes 3076

commit v2 on v1

--- a/solution.py
+++ b/solution.py
@@ -15,8 +15,9 @@
 
 def smooth_kernel(
     nx, ny, rows_i, rows_j,
-    adj_hbm, obj_hbm, rad_hbm, step_hbm, patch_ref, area_ref, jac_ref, orient_ref, count_ref, weight_ref,
+    adj_hbm, obj_hbm, rad_hbm, step_hbm, patch_hbm, area_hbm, jac_hbm, orient_hbm, count_hbm, weight_hbm,
     out_ref, force_ref,
+    patch_ref, area_ref, jac_ref, orient_ref, count_ref, weight_ref,
     adj, one, obj, rad, step, wall, pack1, pack2, halo1, halo2, turned, mine1, mine2, got1, got2,
     load_sem, hsend1, hrecv1, hsend2, hrecv2, psend1, precv1, psend2, precv2,
 ):
@@ -28,13 +29,23 @@
     patch_total = P_DEV * nx * ny
     groups = -(-patch_total // lanes)
 
+    small = [
+        pltpu.make_async_copy(src, dst, load_sem.at[4 + n])
+        for n, (src, dst) in enumerate((
+            (weight_hbm, weight_ref), (count_hbm, count_ref), (patch_hbm, patch_ref), (area_hbm, area_ref),
+            (jac_hbm, jac_ref), (orient_hbm, orient_ref),
+        ))
+    ]
     loads = [
         pltpu.make_async_copy(adj_hbm, adj.at[:, pl.ds(pad, cells), :], load_sem.at[0]),
         pltpu.make_async_copy(obj_hbm, obj, load_sem.at[1]),
         pltpu.make_async_copy(rad_hbm, rad, load_sem.at[2]),
         pltpu.make_async_copy(step_hbm, step, load_sem.at[3]),
     ]
-    for copy in loads:
+    loads[0].start()
+    for copy in small:
+        copy.start()
+    for copy in loads[1:]:
         copy.start()
 
     barrier = pltpu.get_barrier_semaphore()
@@ -92,6 +103,8 @@
     start(first_copies, 2)
     start(first_copies, 3)
 
+    for copy in small:
+        copy.wait()
     weights = [weight_ref[f] for f in range(FIELDS)]
     patch_t = jnp.transpose(patch_ref[...])
     area_t = jnp.transpose(area_ref[...])
@@ -312,7 +325,7 @@
     f32 = jnp.float32
     vmem = pl.BlockSpec(memory_space=pltpu.VMEM)
     smem = pl.BlockSpec(memory_space=pltpu.SMEM)
-    anywhere = pl.BlockSpec(memory_space=pl.ANY)
+    hbm = pl.BlockSpec(memory_space=pltpu.HBM)
     dma = pltpu.SemaphoreType.DMA
     result, force = pl.pallas_call(
         functools.partial(smooth_kernel, nx, ny, rows_i, rows_j),
@@ -320,9 +333,15 @@
             jax.ShapeDtypeStruct((fields, cells, lanes), f32),
             jax.ShapeDtypeStruct((P_DEV,), f32),
         ),
-        in_specs=[anywhere] * 4 + [vmem] * 2 + [smem] * 4,
+        in_specs=[hbm] * 10,
         out_specs=(vmem, smem),
         scratch_shapes=[
+            pltpu.VMEM(face_patch.shape, jnp.int32),
+            pltpu.VMEM(face_area.shape, f32),
+            pltpu.SMEM(flux_jacobian.shape, f32),
+            pltpu.SMEM(face_orient.shape, jnp.int32),
+            pltpu.SMEM(wall_count.shape, jnp.int32),
+            pltpu.SMEM(force_weight.shape, f32),
             pltpu.VMEM((fields, cells + 2 * pad, lanes), f32),
             pltpu.VMEM((fields, cells + 2 * pad, lanes), f32),
             pltpu.VMEM((fields, cells, lanes), f32),
@@ -338,11 +357,11 @@
             pltpu.VMEM((2 * groups, lanes), f32),
             pltpu.VMEM((nx - 1, 2 * groups, lanes), f32),
             pltpu.VMEM((ny - 1, 2 * groups, lanes), f32),
-            dma((4,)), dma((4,)), dma((4,)), dma((4,)), dma((4,)),
+            dma((10,)), dma((4,)), dma((4,)), dma((4,)), dma((4,)),
             dma((nx - 1,)), dma((nx - 1,)), dma((ny - 1,)), dma((ny - 1,)),
         ],
         compiler_params=pltpu.CompilerParams(
-            collective_id=0, has_side_effects=True, vmem_limit_bytes=32 * 1024 * 1024
+            collective_id=0, has_side_effects=True, vmem_limit_bytes=62 * 1024 * 1024
         ),
     )(
         adjoint_start.reshape(fields, cells, lanes),

time: 29.3 us -> 23.3 us (0.80); the launches traced: 28.8 us -> 23.1 us
  local copies, waits for them, and re-layouts: 7.62 us -> 2.61 us
  Pallas kernels: 19.8 us -> 19.1 us
    unnamed x20 -> x4, local copies, waits for them, and re-layouts: 7.62 us -> 2.61 us
    pallas_call x1, Pallas kernels: 19.8 us -> 19.1 us  [local(): pl.pallas_call(functools.partial(smooth_kernel, nx, ny, rows_i, rows_j),...]
where the time goes in v2:
time: 23.3 us; the launch traced here: 23.1 us
  Pallas kernels  19.1 us (82%)
  local copies, waits for them, and re-layouts  2.61 us (11%)
  between operations  1.3 us (6%)
    pallas_call x1, Pallas kernels, local(): pl.pallas_call(functools.partial(smooth_kernel, nx, ny, rows_i, rows_j),...  19.1 us
    unnamed x4, local copies, waits for them, and re-layouts  2.61 us

profile of v2, /device:TPU:0, one launch (start us, length us, event | category | flops | bytes accessed | tf_op | source)
XLA Modules:
  0.0 23.1 jit_solution(2215417608279972578)
XLA Ops:
  1.3 19.1 %shard_map.113 = (f32[6,256,128]{2,1,0:T(8,128)}, f32[4]{0:T(128)}) custom-call(f32[6,256,128]{2,1,0:T(8,128)} %bitcast.5, f32[6,256,128]{2,1,0:T(8,128)} %bitcast.6, f32[3,256,128]{2,1,0:T(8,128)} %bitcast.8, f32[256,128]{1,0:T(8,128)} %bitcast.9, s32[16,16]{1,0:T(8,128)} %patch_hbm.1, f32[16,16]{1,0:T(8,128)} %area_hbm.1, f32[3,6,6]{2,1,0:T(8,128)} %jac_hbm.1, ...), custom_call_target="tpu_custom_call" | custom-call | tf_op jit(solution)/shard_map/pallas_call | solution.py:330
  20.4 0.0 copy-start
  20.4 2.1 %copy.15 = f32[6,16,16,128]{3,2,1,0:T(8,128)} copy(f32[6,16,16,128]{3,2,1,0:T(8,128)} %bitcast.7) | data formatting | bytes 1572864
  22.5 0.0 copy-done
  22.5 0.5 %copy.16 = f32[4]{0:T(128)} copy(f32[4]{0:T(128)S(1)} %copy-done) | data formatting | bytes 32
Async XLA Ops:
  20.4 2.1 %copy-start = (f32[4]{0:T(128)S(1)}, f32[4]{0:T(128)}, u32[]{:S(2)}) copy-start(f32[4]{0:T(128)} %get-tuple-element.9) | copy-start | bytes 52

commit v3 on v2

--- a/solution.py
+++ b/solution.py
@@ -19,6 +19,7 @@
     out_ref, force_ref,
     patch_ref, area_ref, jac_ref, orient_ref, count_ref, weight_ref,
     adj, one, obj, rad, step, wall, pack1, pack2, halo1, halo2, turned, mine1, mine2, got1, got2,
+    shift, rim2, wpack, whalo, wsend, wrecv,
     load_sem, hsend1, hrecv1, hsend2, hrecv2, psend1, precv1, psend2, precv2,
 ):
     cells = rows_i * rows_j
@@ -240,11 +241,15 @@
             target[g, at(edge, offset), :] = target[g, at(edge, offset), :] - size_edge * change
             target[g, at(inner, offset), :] = target[g, at(inner, offset), :] - size_inner * near[g]
 
-    def finish_halo(copies, halo, target, offset, factor):
+    def finish_halo(copies, halo, target, offset, factor, wall_copies=None):
         for s in range(4):
             @pl.when(has[s])
             def _(s=s):
                 copies[s].wait_recv()
+                if wall_copies is not None:
+                    wall_copies[s].wait_recv()
+                    for f in range(FIELDS):
+                        halo[s, f] = halo[s, f] - weights[f] * whalo[s]
                 if s < 2:
                     turn(halo, s, orient_ref[0, s])
                 correct(halo, s, target, offset, factor)
@@ -260,6 +265,15 @@
         copy.start()
     section(adj, one, pad, 0.5, False, half, rows_i)
     finish_halo(first_copies, halo1, one, pad, 0.5)
+    for f in range(FIELDS):
+        rim2[0, f] = one[f, pl.ds(pad, pad), :]
+        rim2[1, f] = one[f, pl.ds(cells, pad), :]
+    second_copies = halo_copies(rim2.at[0], rim2.at[1], pack2, halo2, hsend2, hrecv2)
+    start(second_copies, 0)
+    start(second_copies, 1)
+    pack_faces(one, pack2)
+    start(second_copies, 2)
+    start(second_copies, 3)
     for copy in y_copies:
         copy.wait_recv()
     summed = functools.reduce(lambda a, b: a + b, [got2[o] for o in range(ny - 1)], mine2[...])
@@ -274,18 +288,24 @@
         face = jnp.where(lane == 0, face, 0.0)
         wall[pl.ds(i * rows_j, rows_j), :] = face
         moved = 0.5 * step[pl.ds(i * rows_j, rows_j), :] * face
+        shift[pl.ds(i * rows_j, rows_j), :] = moved
         for f in range(FIELDS):
             at = pl.ds(pad + i * rows_j, rows_j)
             one[f, at, :] = one[f, at, :] - weights[f] * moved
 
-    second_copies = halo_copies(
-        one.at[:, pl.ds(pad, pad), :], one.at[:, pl.ds(cells, pad), :], pack2, halo2, hsend2, hrecv2
-    )
-    start(second_copies, 0)
-    start(second_copies, 1)
-    pack_faces(one, pack2)
-    start(second_copies, 2)
-    start(second_copies, 3)
+    for side, first in ((0, 0), (1, rows_j - 2)):
+        for layer in range(2):
+            wpack[side, pl.ds(layer * rows_i, rows_i), :] = shift[pl.ds(first + layer, rows_i, stride=rows_j), :]
+    wall_sources = [shift.at[pl.ds(cells - pad, pad), :], shift.at[pl.ds(0, pad), :], wpack.at[1], wpack.at[0]]
+    wall_copies = [
+        pltpu.make_async_remote_copy(
+            src_ref=wall_sources[s], dst_ref=whalo.at[s], send_sem=wsend.at[s], recv_sem=wrecv.at[s],
+            device_id=targets[s], device_id_type=MESH,
+        )
+        for s in range(4)
+    ]
+    for s in range(4):
+        start(wall_copies, s)
 
     own = (at_x * ny + at_y) * P_DEV
     place = lax.broadcasted_iota(jnp.int32, (groups, lanes), 0) * lanes + lax.broadcasted_iota(
@@ -295,9 +315,9 @@
         force_ref[q] = jnp.sum(jnp.where(place == own + q, force, 0.0))
 
     section(one, out_ref, 0, 1.0, True, 0, rows_i)
-    finish_halo(second_copies, halo2, out_ref, 0, 1.0)
-
-    for copies in (first_copies, second_copies):
+    finish_halo(second_copies, halo2, out_ref, 0, 1.0, wall_copies)
+
+    for copies in (first_copies, second_copies, wall_copies):
         for s in range(4):
             @pl.when(source_has[s])
             def _(s=s, copies=copies):
@@ -330,7 +350,7 @@
     result, force = pl.pallas_call(
         functools.partial(smooth_kernel, nx, ny, rows_i, rows_j),
         out_shape=(
-            jax.ShapeDtypeStruct((fields, cells, lanes), f32),
+            pltpu.VMEM((fields, cells, lanes), f32),
             jax.ShapeDtypeStruct((P_DEV,), f32),
         ),
         in_specs=[hbm] * 10,
@@ -357,6 +377,11 @@
             pltpu.VMEM((2 * groups, lanes), f32),
             pltpu.VMEM((nx - 1, 2 * groups, lanes), f32),
             pltpu.VMEM((ny - 1, 2 * groups, lanes), f32),
+            pltpu.VMEM((cells, lanes), f32),
+            pltpu.VMEM((2, fields, pad, lanes), f32),
+            pltpu.VMEM((2, 2 * rows_i, lanes), f32),
+            pltpu.VMEM((4, pad, lanes), f32),
+            dma((4,)), dma((4,)),
             dma((10,)), dma((4,)), dma((4,)), dma((4,)), dma((4,)),
             dma((nx - 1,)), dma((nx - 1,)), dma((ny - 1,)), dma((ny - 1,)),
         ],

time: 23.3 us -> 21.3 us (0.914)
  local copies, waits for them, and re-layouts: 2.61 us -> 1.4 us
  Pallas kernels: 19.1 us -> 18.4 us
    unnamed x4, local copies, waits for them, and re-layouts: 2.61 us -> 1.4 us
    pallas_call x1, Pallas kernels: 19.1 us -> 18.4 us  [local(): pl.pallas_call(functools.partial(smooth_kernel, nx, ny, rows_i, rows_j),...]
where the time goes in v3:
time: 21.3 us; the launch traced here: 21.1 us
  Pallas kernels  18.4 us (86%)
  local copies, waits for them, and re-layouts  1.4 us (7%)
  between operations  1.3 us (6%)
    pallas_call x1, Pallas kernels, local(): pl.pallas_call(functools.partial(smooth_kernel, nx, ny, rows_i, rows_j),...  18.4 us
    unnamed x4, local copies, waits for them, and re-layouts  1.4 us

profile of v3, /device:TPU:0, one launch (start us, length us, event | category | flops | bytes accessed | tf_op | source)
XLA Modules:
  0.0 21.1 jit_solution(9403570018306725288)
XLA Ops:
  1.3 18.4 %shard_map.113 = (f32[6,256,128]{2,1,0:T(8,128)S(1)}, f32[4]{0:T(128)}) custom-call(f32[6,256,128]{2,1,0:T(8,128)} %bitcast.6, f32[6,256,128]{2,1,0:T(8,128)} %bitcast.7, f32[3,256,128]{2,1,0:T(8,128)} %bitcast.8, f32[256,128]{1,0:T(8,128)} %bitcast.9, s32[16,16]{1,0:T(8,128)} %patch_hbm.1, f32[16,16]{1,0:T(8,128)} %area_hbm.1, f32[3,6,6]{2,1,0:T(8,128)} %jac_hbm.1, ...), custom_call_target="tpu_custom_call" | custom-call | tf_op jit(solution)/shard_map/pallas_call | solution.py:350
  19.7 0.0 copy-start
  19.7 0.9 %copy.14 = f32[6,16,16,128]{3,2,1,0:T(8,128)} copy(f32[6,16,16,128]{3,2,1,0:T(8,128)S(1)} %bitcast.5) | data formatting | bytes 1572864
  20.6 0.0 copy-done
  20.6 0.5 %copy.16 = f32[4]{0:T(128)} copy(f32[4]{0:T(128)S(1)} %copy-done) | data formatting | bytes 32
Async XLA Ops:
  19.7 0.9 %copy-start = (f32[4]{0:T(128)S(1)}, f32[4]{0:T(128)}, u32[]{:S(2)}) copy-start(f32[4]{0:T(128)} %get-tuple-element.11) | copy-start | bytes 52
